TPU v7x, 128 devices: a whole 4x4x4 slice. The times are simulated.
128 devices in a mesh: gx: 4 (over y), gy: 32 (over z, x, core).
Axes of the slice: x: 4, y: 4, z: 4, core: 2. Of those that a mesh axis runs over, the one named last changes fastest.
Arguments:
- grid_latent: bfloat16 [32768, 512], P(('gx', 'gy')), may hold values from -6 to 6
- mesh_latent: bfloat16 [16384, 512], P(('gx', 'gy')), may hold values from -6 to 6
- w_grid: bfloat16 [512, 512], replicated, may hold values from -0.25 to 0.25
- w_recv: bfloat16 [512, 512], replicated, may hold values from -0.25 to 0.25
- w_send: bfloat16 [512, 512], replicated, may hold values from -0.25 to 0.25
- w_node: bfloat16 [512, 512], replicated, may hold values from -0.25 to 0.25
- encode_sender: int32 [49152], P(('gx', 'gy')), may hold values from 0 to 255
- encode_owner: int32 [49152, 1], P(('gx', 'gy')), may hold values from 0 to 127; in each aligned block of 384 rows (0 to 383, 384 to 767, ...) at most 9 rows name the same one
- encode_target: int32 [49152], P(('gx', 'gy')), may hold values from 0 to 127
- mesh_sender: int32 [65536], P(('gx', 'gy')), may hold values from 0 to 127
- mesh_owner: int32 [65536, 1], P(('gx', 'gy')), may hold values from 0 to 127; in each aligned block of 512 rows (0 to 511, 512 to 1023, ...) at most 12 rows name the same one
- mesh_target: int32 [65536], P(('gx', 'gy')), may hold values from 0 to 127
- cotangent: bfloat16 [16384, 512], P(('gx', 'gy')), may hold values from -6 to 6
Outputs:
- mesh_out: bfloat16 [16384, 512], P(('gx', 'gy'))
- grid_grad: bfloat16 [32768, 512], P(('gx', 'gy'))
- mesh_grad: bfloat16 [16384, 512], P(('gx', 'gy'))
Inputs may be any that keep to these rules, and one draw needn't show every extreme that they name: `encode_owner`: in the edges of one device, at most 9 name one owner, and some device names some owner exactly 9 times. `mesh_owner`: in the edges of one device, at most 12 name one owner, and some device names some owner exactly 12 times.
All inputs are finite; a program needn't handle non-finite values.
Results may differ from a plain program's by a relative error of at most 0.02.
Values may be sent and summed in bfloat16 or wider, within the bound.
A program may use at most 128 MiB of HBM per device.

v0:
```python
import functools

import jax
import jax.numpy as jnp
from jax import lax
from jax.experimental import pallas as pl
from jax.experimental.pallas import tpu as pltpu
from jax.sharding import PartitionSpec as P

MESH = pl.DeviceIdType.MESH
BF = jnp.bfloat16
F32 = jnp.float32
I32 = jnp.int32

PEERS = 128
GROUPS = 8
SIZE = 16
MAIN = SIZE * 8
TAIL = SIZE * 4
ROWS = MAIN + TAIL
UNITS = 48
FORTH, BACK = 37, 45


def coords():
    y = lax.axis_index("gx")
    g = lax.axis_index("gy")
    return y, g // 8, (g // 2) % 4, g % 2


def partner(j, sign):
    y, z, x, c = coords()
    i = (j * FORTH) % PEERS
    dy, dz, dx, dc = i // 32, (i // 8) % 4, (i // 2) % 4, i % 2
    if sign < 0:
        dy, dz, dx = 4 - dy, 4 - dz, 4 - dx
    return (y + dy) % 4, ((z + dz) % 4) * 8 + ((x + dx) % 4) * 2 + (c + dc) % 2


def iota(shape, axis):
    return lax.broadcasted_iota(I32, shape, axis)


def onehot(mask):
    return jnp.where(mask, 1.0, 0.0).astype(BF)


def mm(a, b):
    return lax.dot_general(a, b, (((1,), (0,)), ((), ())), preferred_element_type=F32)


def mm_nt(a, b):
    return lax.dot_general(a, b, (((1,), (1,)), ((), ())), preferred_element_type=F32)


def swap(a, b):
    low = iota(a.shape, 1) < 4
    return jnp.where(low, a, pltpu.roll(b, 4, 1)), jnp.where(low, pltpu.roll(a, 4, 1), b)


def pack(wire, g, rows):
    at = pl.ds(g * SIZE, SIZE)
    m = [rows[:MAIN, c * 128 : c * 128 + 128].reshape(SIZE, 8, 128) for c in range(4)]
    t = [rows[MAIN:, c * 128 : c * 128 + 128].reshape(SIZE // 2, 8, 128) for c in range(4)]
    wire[at, 0:16, :] = jnp.concatenate([m[0], m[1]], axis=1).astype(BF)
    wire[at, 16:32, :] = jnp.concatenate([m[2], m[3]], axis=1).astype(BF)
    e01, o01 = swap(t[0], t[1])
    e23, o23 = swap(t[2], t[3])
    even = jnp.concatenate([e01, e23], axis=1)
    odd = jnp.concatenate([o01, o23], axis=1)
    wire[at, 32:48, :] = jnp.stack([even, odd], axis=1).reshape(SIZE, 16, 128).astype(BF)


def unpack(wire, g):
    at = pl.ds(g * SIZE, SIZE)
    a = wire[at, 0:16, :].astype(F32)
    b = wire[at, 16:32, :].astype(F32)
    t = wire[at, 32:48, :].astype(F32).reshape(SIZE // 2, 2, 16, 128)
    even, odd = t[:, 0], t[:, 1]
    t0, t1 = swap(even[:, :8], odd[:, :8])
    t2, t3 = swap(even[:, 8:], odd[:, 8:])
    main = [v.reshape(MAIN, 128) for v in (a[:, :8], a[:, 8:], b[:, :8], b[:, 8:])]
    tail = [v.reshape(TAIL, 128) for v in (t0, t1, t2, t3)]
    return jnp.concatenate(
        [jnp.concatenate(main, axis=1), jnp.concatenate(tail, axis=1)], axis=0
    )


def norm_forward(total):
    scale = lax.rsqrt(jnp.mean(total * total, axis=-1, keepdims=True) + 1e-05)
    return total * scale, scale


def norm_backward(grad, total, scale):
    inner = jnp.mean(grad * total, axis=-1, keepdims=True)
    return scale * (grad - total * (scale * scale * inner))


def kernel(
    grid_ref,
    mesh_ref,
    w_grid,
    w_recv,
    w_send,
    w_node,
    es,
    eo,
    et,
    ms,
    mo,
    mt,
    cot,
    out_ref,
    grid_grad,
    mesh_grad,
    send1,
    recv1,
    send2,
    recv2,
    back2,
    ret2,
    back1,
    ret1,
    a1,
    a1t,
    a2,
    a2t,
    r1,
    r1t,
    r2,
    r2t,
    d1,
    d2,
    tm,
    rows1,
    gathered,
    total,
    hidden_ref,
    ssem,
    rsem,
):
    barrier = pltpu.get_barrier_semaphore()

    def signal(j, carry):
        ty, tg = partner(j, 1)
        pl.semaphore_signal(barrier, inc=1, device_id=(ty, tg), device_id_type=MESH)
        return carry

    lax.fori_loop(1, PEERS, signal, 0)

    y, z, x, c = coords()

    def route(owner):
        edges = owner.shape[1]
        dy = ((owner >> 5) - y) & 3
        dz = (((owner >> 3) & 3) - z) & 3
        dx = (((owner >> 1) & 3) - x) & 3
        dc = ((owner & 1) - c) & 1
        j = ((dy * 32 + dz * 8 + dx * 2 + dc) * BACK) & 127
        same = iota((PEERS, edges), 0) == j
        before = onehot(iota((edges, edges), 0) < iota((edges, edges), 1))
        count = mm(onehot(same), before)
        rank = jnp.sum(jnp.where(same, count, 0.0), axis=0, keepdims=True).astype(I32)
        return j, rank, onehot(same)

    def slots(j, rank):
        inside = jnp.where(rank < 8, (j & 15) * 8 + rank, MAIN + (j & 15) * 4 + rank - 8)
        return (j >> 4) * ROWS + inside

    def labels(rank, target, base):
        at = iota((128, rank.shape[1]), 0) == rank + base
        return jnp.where(at, (target + 1).astype(F32), 0.0).astype(BF)

    def selectors(place, sender, nodes, a, at):
        edges = place.shape[1]
        q = onehot(iota((nodes, edges), 0) == sender)
        for g in range(GROUPS):
            p = onehot(iota((ROWS, edges), 0) + g * ROWS == place)
            a[g] = mm_nt(p, q).astype(BF)
            at[g] = mm_nt(q, p).astype(BF)

    j1, k1, same1 = route(eo[...])
    j2, k2, same2 = route(mo[...])
    tm[...] = (
        mm_nt(same1, labels(k1, et[...], 0)) + mm_nt(same2, labels(k2, mt[...], 16))
    ).astype(BF)
    selectors(slots(j1, k1), es[...], grid_ref.shape[0], a1, a1t)
    selectors(slots(j2, k2), ms[...], mesh_ref.shape[0], a2, a2t)
    rows1[...] = mm(grid_ref[...], w_grid[...]).astype(BF)
    gathered[...] = mm(mesh_ref[...], w_recv[...]).astype(BF)

    pl.semaphore_wait(barrier, PEERS - 1)

    def send_group(g, phase, src, dst, sign):
        def one(k, carry):
            j = g * SIZE + k
            ty, tg = partner(j, sign)
            pltpu.make_async_remote_copy(
                src.at[j],
                dst.at[j],
                ssem.at[phase],
                rsem.at[phase, g],
                device_id=(ty, tg),
                device_id_type=MESH,
            ).start()
            return carry

        @pl.when(g == 0)
        def _():
            pltpu.make_async_copy(src.at[0], dst.at[0], rsem.at[phase, 0]).start()
            lax.fori_loop(1, SIZE, one, 0)

        @pl.when(g > 0)
        def _():
            lax.fori_loop(0, SIZE, one, 0)

    def wait_group(g, phase, dst):
        at = dst.at[pl.ds(g * SIZE, SIZE)]
        pltpu.make_async_copy(at, at, rsem.at[phase, g]).wait()

    slot_r = iota((ROWS, SIZE), 0)
    peer_r = iota((ROWS, SIZE), 1)
    slot_c = iota((SIZE, ROWS), 1)
    peer_c = iota((SIZE, ROWS), 0)

    def peer_of(s):
        return jnp.where(s < MAIN, s >> 3, (s - MAIN) >> 2)

    def rank_of(s):
        return jnp.where(s < MAIN, s & 7, 8 + (s & 3))

    mark = onehot((slot_r == MAIN + 4 * peer_r + 1))
    unmark = onehot((slot_c == MAIN + 4 * peer_c + 1))
    spread = onehot(peer_of(slot_c) == peer_c)
    eye128 = onehot(iota((128, 128), 0) == iota((128, 128), 1))
    eye_rows = onehot(iota((ROWS, ROWS), 0) == iota((ROWS, ROWS), 1))
    rank_c = rank_of(iota((128, ROWS), 1))
    lane_of = iota((128, ROWS), 0)

    def send_enc(g, carry):
        rows = mm(a1[g], rows1[...])
        label = mm(mark, tm[pl.ds(pl.multiple_of(g * SIZE, SIZE), SIZE), :])
        rows = jnp.concatenate([rows[:, :128] + label, rows[:, 128:]], axis=1)
        pack(send1, g, rows)
        send_group(g, 0, send1, recv1, 1)
        return carry

    lax.fori_loop(0, GROUPS, send_enc, 0)

    def message(g, rows, r, rt, d):
        pre = rows + mm(r[g], gathered[...])
        gate = 0.5 * jnp.tanh(0.5 * pre) + 0.5
        value = pre * gate
        d[g] = (gate + value * (1.0 - gate)).astype(BF)
        total[...] += mm(rt[g], value.astype(BF))

    total[...] = jnp.zeros_like(total)

    def take_enc(g, carry):
        wait_group(g, 0, recv1)
        rows = unpack(recv1, g)
        mine = mm(unmark, rows[:, :128].astype(BF)).astype(BF)
        mine_t = mm_nt(eye128, mine).astype(BF)
        lines = mm(mine_t, spread)
        for base, r, rt in ((0, r1, r1t), (16, r2, r2t)):
            row = jnp.sum(
                jnp.where(lane_of == rank_c + base, lines, 0.0), axis=0, keepdims=True
            )
            flag = onehot(row.astype(I32) == lane_of + 1)
            rt[g] = flag
            r[g] = mm_nt(eye_rows, flag).astype(BF)
        message(g, rows, r1, r1t, d1)
        return carry

    lax.fori_loop(0, GROUPS, take_enc, 0)

    enc_sum = total[...]
    enc_norm, enc_scale = norm_forward(enc_sum)
    hidden = mesh_ref[...].astype(F32) + mm(enc_norm.astype(BF), w_node[...])
    hidden_ref[...] = hidden
    hidden_bf = hidden.astype(BF)
    sent = mm(hidden_bf, w_send[...]).astype(BF)
    rows1[pl.ds(0, 128), :] = sent

    def send_msh(g, carry):
        pack(send2, g, mm(a2[g], rows1[pl.ds(0, 128), :]))
        send_group(g, 1, send2, recv2, 1)
        return carry

    lax.fori_loop(0, GROUPS, send_msh, 0)
    gathered[...] = mm(hidden_bf, w_recv[...]).astype(BF)
    total[...] = jnp.zeros_like(total)

    def take_msh(g, carry):
        wait_group(g, 1, recv2)
        message(g, unpack(recv2, g), r2, r2t, d2)
        return carry

    lax.fori_loop(0, GROUPS, take_msh, 0)

    msh_sum = total[...]
    msh_norm, msh_scale = norm_forward(msh_sum)
    cot_bf = cot[...]
    grad_norm = mm_nt(cot_bf, w_node[...]).astype(BF).astype(F32)
    gathered[...] = norm_backward(grad_norm, msh_sum, msh_scale).astype(BF)

    total[...] = jnp.zeros_like(total)

    def grad_group(g, phase, r, rt, d, back, ret):
        grad = mm(r[g], gathered[...]) * d[g].astype(F32)
        pack(back, g, grad)
        send_group(g, phase, back, ret, -1)
        total[...] += mm(rt[g], grad.astype(BF))

    def back_msh(g, carry):
        grad_group(g, 2, r2, r2t, d2, back2, ret2)
        return carry

    lax.fori_loop(0, GROUPS, back_msh, 0)
    out_ref[...] = (hidden_ref[...] + mm(msh_norm.astype(BF), w_node[...])).astype(BF)
    grad_recv = total[...].astype(BF)
    part = mm_nt(grad_recv, w_recv[...])
    total[...] = jnp.zeros_like(total)

    def take_back_msh(g, carry):
        wait_group(g, 2, ret2)
        total[...] += mm(a2t[g], unpack(ret2, g).astype(BF))
        return carry

    lax.fori_loop(0, GROUPS, take_back_msh, 0)
    grad_hidden_bf = (part + mm_nt(total[...].astype(BF), w_send[...])).astype(BF)
    grad_hidden = (cot_bf.astype(F32) + grad_hidden_bf.astype(F32)).astype(BF)
    grad_norm1 = mm_nt(grad_hidden, w_node[...]).astype(BF).astype(F32)
    gathered[...] = norm_backward(grad_norm1, enc_sum, enc_scale).astype(BF)

    total[...] = jnp.zeros_like(total)

    def back_enc(g, carry):
        grad_group(g, 3, r1, r1t, d1, back1, ret1)
        return carry

    lax.fori_loop(0, GROUPS, back_enc, 0)
    mesh_part = mm_nt(total[...].astype(BF), w_recv[...]).astype(BF)
    mesh_grad[...] = (grad_hidden.astype(F32) + mesh_part.astype(F32)).astype(BF)

    def take_back_enc(g, carry):
        wait_group(g, 3, ret1)
        return carry + mm(a1t[g], unpack(ret1, g).astype(BF))

    grid_rows = lax.fori_loop(
        0, GROUPS, take_back_enc, jnp.zeros(grid_ref.shape, F32)
    )
    grid_grad[...] = mm_nt(grid_rows.astype(BF), w_grid[...]).astype(BF)

    for phase, src in enumerate((send1, send2, back2, back1)):
        at = src.at[pl.ds(1, PEERS - 1)]
        pltpu.make_async_copy(at, at, ssem.at[phase]).wait()


def body(
    grid_latent,
    mesh_latent,
    w_grid,
    w_recv,
    w_send,
    w_node,
    encode_sender,
    encode_owner,
    encode_target,
    mesh_sender,
    mesh_owner,
    mesh_target,
    cotangent,
):
    vmem = pl.BlockSpec(memory_space=pltpu.VMEM)
    wire = pltpu.VMEM((PEERS, UNITS, 128), BF)
    nodes, width = mesh_latent.shape
    grid_nodes = grid_latent.shape[0]
    scratch = (
        [wire] * 8
        + [
            pltpu.VMEM((GROUPS, ROWS, grid_nodes), BF),
            pltpu.VMEM((GROUPS, grid_nodes, ROWS), BF),
            pltpu.VMEM((GROUPS, ROWS, nodes), BF),
            pltpu.VMEM((GROUPS, nodes, ROWS), BF),
        ]
        + [pltpu.VMEM((GROUPS, ROWS, nodes), BF), pltpu.VMEM((GROUPS, nodes, ROWS), BF)] * 2
        + [pltpu.VMEM((GROUPS, ROWS, width), BF)] * 2
        + [
            pltpu.VMEM((PEERS, 128), BF),
            pltpu.VMEM((grid_nodes, width), BF),
            pltpu.VMEM((nodes, width), BF),
            pltpu.VMEM((nodes, width), F32),
            pltpu.VMEM((nodes, width), F32),
            pltpu.SemaphoreType.DMA((4,)),
            pltpu.SemaphoreType.DMA((4, GROUPS)),
        ]
    )
    row = lambda v: v.reshape(1, -1)
    return pl.pallas_call(
        kernel,
        out_shape=(
            jax.ShapeDtypeStruct(mesh_latent.shape, BF),
            jax.ShapeDtypeStruct(grid_latent.shape, BF),
            jax.ShapeDtypeStruct(mesh_latent.shape, BF),
        ),
        in_specs=[vmem] * 13,
        out_specs=[vmem] * 3,
        scratch_shapes=scratch,
        compiler_params=pltpu.CompilerParams(
            collective_id=0, has_side_effects=True, vmem_limit_bytes=56 << 20
        ),
    )(
        grid_latent,
        mesh_latent,
        w_grid,
        w_recv,
        w_send,
        w_node,
        row(encode_sender),
        row(encode_owner),
        row(encode_target),
        row(mesh_sender),
        row(mesh_owner),
        row(mesh_target),
        cotangent,
    )


def solution(mesh):
    rows = P(("gx", "gy"), None)
    flat = P(("gx", "gy"))
    placed = (rows, rows, P(), P(), P(), P(), flat, rows, flat, flat, rows, flat, rows)
    return jax.shard_map(
        body, mesh=mesh, in_specs=placed, out_specs=(rows, rows, rows), check_vma=False
    )
```

profile of v0, /device:TPU:1, one launch (start us, length us, event | category | flops | bytes accessed | tf_op | source)
XLA Modules:
  0.0 113.7 jit_solution(1936849523903028316)
XLA Ops:
  0.6 0.0 copy-start.2
  0.6 0.7 copy-done.2
  1.3 0.0 copy-start.3
  1.3 0.6 reshape.24.es
  1.9 0.1 copy-done.3
  2.0 0.6 reshape.26.et
  2.6 107.9 %shard_map.148 = (bf16[128,512]{1,0:T(8,128)(2,1)}, bf16[256,512]{1,0:T(8,128)(2,1)}, bf16[128,512]{1,0:T(8,128)(2,1)}) custom-call(bf16[256,512]{1,0:T(8,128)(2,1)} %grid_ref.1, bf16[128,512]{1,0:T(8,128)(2,1)} %mesh_ref.1, bf16[512,512]{1,0:T(8,128)(2,1)} %w_grid.1, bf16[512,512]{1,0:T(8,128)(2,1)} %w_recv.1, bf16[512,512]{1,0:T(8,128)(2,1)} %w_send.1, ...), custom_call_target="tpu_custom_call" | custom-call | tf_op jit(solution)/shard_map/pallas_call | solution.py:400
  110.5 0.0 copy-start
  110.5 1.6 %copy.19 = bf16[128,512]{1,0:T(8,128)(2,1)} copy(bf16[128,512]{1,0:T(8,128)(2,1)} %get-tuple-element.6) | data formatting | bytes 262144
  112.1 0.0 copy-done
  112.1 0.0 copy-start.1
  112.1 0.7 copy.20
  112.8 0.3 copy-done.1
  113.1 0.7 copy.21
Async XLA Ops:
  0.6 0.7 copy-start.2
  1.3 0.7 copy-start.3
  110.5 1.6 %copy-start = (bf16[256,512]{1,0:T(8,128)(2,1)S(1)}, bf16[256,512]{1,0:T(8,128)(2,1)}, u32[]{:S(2)}) copy-start(bf16[256,512]{1,0:T(8,128)(2,1)} %get-tuple-element.7) | copy-start | bytes 786436
  112.1 1.0 copy-start.1
where the time goes:
time: 114 us
  Pallas kernels  108 us (95%)
  local copies, waits for them, and re-layouts  5.19 us (5%)
    pallas_call x1, Pallas kernels, body(): pl.pallas_call(kernel, out_shape=(jax.ShapeDtypeStruct(mesh_latent.shape,...  108 us
    unnamed x11, local copies, waits for them, and re-layouts  4.06 us

commit v1 on v0

v1 whole, which is shorter than its diff:
```python
import jax
import jax.numpy as jnp
from jax import lax
from jax.experimental import pallas as pl
from jax.experimental.pallas import tpu as pltpu
from jax.sharding import PartitionSpec as P

MESH = pl.DeviceIdType.MESH
BF = jnp.bfloat16
F32 = jnp.float32
I32 = jnp.int32

PEERS = 128
GROUPS = 8
SIZE = 16
MAIN = SIZE * 8
TAIL = SIZE * 4
LAST = SIZE * 8
ROWS1 = MAIN + LAST
ROWS2 = MAIN + TAIL
NEVER = 99


def coords():
    y = lax.axis_index("gx")
    g = lax.axis_index("gy")
    return y, g // 8, (g // 2) % 4, g % 2


def iota(shape, axis):
    return lax.broadcasted_iota(I32, shape, axis)


def onehot(mask):
    return jnp.where(mask, 1.0, 0.0).astype(BF)


def mm(a, b):
    return lax.dot_general(a, b, (((1,), (0,)), ((), ())), preferred_element_type=F32)


def mm_nt(a, b):
    return lax.dot_general(a, b, (((1,), (1,)), ((), ())), preferred_element_type=F32)


def quarter(v, q):
    return v[..., q * 128 : q * 128 + 128]


def swap(a, b):
    low = iota(a.shape, 1) < 4
    return jnp.where(low, a, pltpu.roll(b, 4, 1)), jnp.where(low, pltpu.roll(a, 4, 1), b)


def pack_main(wire, g, rows):
    at = pl.ds(g * SIZE, SIZE)
    m = [quarter(rows, q).reshape(SIZE, 8, 128) for q in range(4)]
    wire[at, 0:16, :] = jnp.concatenate([m[0], m[1]], axis=1).astype(BF)
    wire[at, 16:32, :] = jnp.concatenate([m[2], m[3]], axis=1).astype(BF)


def unpack_main(wire, g):
    at = pl.ds(g * SIZE, SIZE)
    a = wire[at, 0:16, :].astype(F32)
    b = wire[at, 16:32, :].astype(F32)
    parts = (a[:, :8], a[:, 8:], b[:, :8], b[:, 8:])
    return jnp.concatenate([v.reshape(MAIN, 128) for v in parts], axis=1)


def pack_tail(wire, g, rows):
    t = [quarter(rows, q).reshape(SIZE // 2, 8, 128) for q in range(4)]
    e01, o01 = swap(t[0], t[1])
    e23, o23 = swap(t[2], t[3])
    even = jnp.concatenate([e01, e23], axis=1)
    odd = jnp.concatenate([o01, o23], axis=1)
    both = jnp.stack([even, odd], axis=1).reshape(SIZE, 16, 128)
    wire[pl.ds(g * SIZE, SIZE), 32:48, :] = both.astype(BF)


def unpack_tail(wire, g):
    t = wire[pl.ds(g * SIZE, SIZE), 32:48, :].astype(F32).reshape(SIZE // 2, 2, 16, 128)
    even, odd = t[:, 0], t[:, 1]
    t0, t1 = swap(even[:, :8], odd[:, :8])
    t2, t3 = swap(even[:, 8:], odd[:, 8:])
    return jnp.concatenate([v.reshape(TAIL, 128) for v in (t0, t1, t2, t3)], axis=1)


def pack(wire, g, rows):
    pack_main(wire, g, rows[:MAIN])
    pack_tail(wire, g, rows[MAIN:])


def unpack(wire, g):
    return jnp.concatenate([unpack_main(wire, g), unpack_tail(wire, g)], axis=0)


def fold(rows):
    u = iota((LAST, 128), 0) & 7
    part = jnp.where(u == 2, quarter(rows, 2), quarter(rows, 3))
    return jnp.where(u == 0, quarter(rows, 0), jnp.where(u == 1, quarter(rows, 1), part))


def unfold(part):
    u = iota((LAST, 128), 0) & 7
    return jnp.concatenate([jnp.where(u == q, part, 0.0) for q in range(4)], axis=1)


def norm_forward(total):
    scale = lax.rsqrt(jnp.mean(total * total, axis=-1, keepdims=True) + 1e-05)
    return total * scale, scale


def norm_backward(grad, total, scale):
    inner = jnp.mean(grad * total, axis=-1, keepdims=True)
    return scale * (grad - total * (scale * scale * inner))


def gated(pre):
    gate = 0.5 * jnp.tanh(0.5 * pre) + 0.5
    value = pre * gate
    return value, gate + value * (1.0 - gate)


def kernel(*refs):
    inputs, refs = refs[:13], refs[13:]
    (out_ref, grid_grad, mesh_grad), refs = refs[:3], refs[3:]
    local, refs = refs[:13], refs[13:]
    grid_ref, mesh_ref, w_grid, w_recv, w_send, w_node, es, eo, et, ms, mo, mt, cot = local
    (
        send1, last1, recv1, rlast1, send2, recv2, back2, ret2, back1, blast1, ret1, tlast1,
        a1, a1t, a2, a2t, r1, r1t, r2, r2t, d1, d1l, d2,
        tm, rows1, gathered, total, hidden_ref,
        isem, ssem, rsem, lsem, zsem, ysem,
    ) = refs

    y, z, x, c = coords()
    gy = z * 8 + x * 2 + c

    loads = [pltpu.make_async_copy(a, b, isem.at[n]) for n, (a, b) in enumerate(zip(inputs, local))]
    order = (7, 10, 8, 11, 6, 9, 0, 2, 1, 3, 5, 4, 12)
    for n in order:
        loads[n].start()

    barrier = pltpu.get_barrier_semaphore()
    ring_x = [(y, z * 8 + ((x + d // 2) % 4) * 2 + (c + d) % 2) for d in range(1, 8)]
    ring_z = [(y, ((z + d) % 4) * 8 + x * 2 + c) for d in range(1, 4)]
    ring_y = [((y + d) % 4, gy) for d in range(1, 4)]

    def greet(sem, ring):
        for device in ring:
            pl.semaphore_signal(sem, inc=1, device_id=device, device_id_type=MESH)

    greet(barrier, ring_x + ring_z + ring_y)

    def route(owner):
        edges = owner.shape[1]
        dy = ((owner >> 5) - y) & 3
        dz = (((owner >> 3) & 3) - z) & 3
        dx = (((owner >> 1) & 3) - x) & 3
        dc = ((owner & 1) - c) & 1
        j = (((dy - dz - dx) & 3) * 2 + dc) * SIZE + dz * 4 + dx
        same = iota((PEERS, edges), 0) == j
        before = onehot(iota((edges, edges), 0) < iota((edges, edges), 1))
        count = mm(onehot(same), before)
        rank = jnp.sum(jnp.where(same, count, 0.0), axis=0, keepdims=True).astype(I32)
        return j, rank, onehot(same)

    def labels(rank, target, base):
        at = iota((128, rank.shape[1]), 0) == rank + base
        return jnp.where(at, (target + 1).astype(F32), 0.0).astype(BF)

    for n in (7, 10, 8, 11):
        loads[n].wait()
    j1, k1, same1 = route(eo[...])
    j2, k2, same2 = route(mo[...])
    tm[...] = (
        mm_nt(same1, labels(k1, et[...].reshape(1, -1), 0)) + mm_nt(same2, labels(k2, mt[...].reshape(1, -1), 16))
    ).astype(BF)

    pl.semaphore_wait(barrier, 13)
    greet(zsem, ring_z)

    loads[6].wait()
    edges1 = j1.shape[1]
    q1 = onehot(iota((grid_ref.shape[0], edges1), 0) == es[...].reshape(1, -1))
    main1 = jnp.where(k1 < 8, j1 * 8 + k1, -1)
    last1_of = jnp.where(k1 == 8, j1, -1)
    row1 = iota((MAIN, edges1), 0)
    for g in range(GROUPS):
        p_main = onehot(row1 + g * MAIN == main1)
        p_last = onehot(jnp.where((row1 & 7) < 4, (row1 >> 3) + g * SIZE, -2) == last1_of)
        p = jnp.concatenate([p_main, p_last], axis=0)
        a1[g] = mm_nt(p, q1).astype(BF)
        a1t[g] = mm_nt(q1, p).astype(BF)

    pl.semaphore_wait(zsem, 3)
    greet(ysem, ring_y)

    for n in (0, 2):
        loads[n].wait()
    rows1[...] = mm(grid_ref[...], w_grid[...]).astype(BF)
    for n in (1, 3):
        loads[n].wait()
    gathered[...] = mm(mesh_ref[...], w_recv[...]).astype(BF)

    pl.semaphore_wait(ysem, 3)

    def send_group(g, phase, wires, sign):
        gh, gl = g // 2, g % 2
        tc = (c + gl) % 2
        ty = [(y + sign * (gh + m) + 8) % 4 for m in range(4)]
        for k in range(SIZE):
            kz, kx = k // 4, k % 4
            tz, tx = (z + sign * kz + 4) % 4, (x + sign * kx + 4) % 4
            device = (ty[(kz + kx) % 4], tz * 8 + tx * 2 + tc)
            j = g * SIZE + k

            def remote():
                for src, dst, s, r in wires:
                    pltpu.make_async_remote_copy(
                        src.at[j], dst.at[j], s, r, device_id=device, device_id_type=MESH
                    ).start()

            def mine():
                for src, dst, s, r in wires:
                    pltpu.make_async_copy(src.at[j], dst.at[j], r).start()

            if k == 0:
                pl.when(g > 0)(remote)
                pl.when(g == 0)(mine)
            else:
                remote()

    def wait_group(g, dst, sem):
        at = dst.at[pl.ds(g * SIZE, SIZE)]
        pltpu.make_async_copy(at, at, sem).wait()

    mark = onehot(iota((LAST, SIZE), 0) == 8 * iota((LAST, SIZE), 1) + 4)
    unmark = onehot(iota((SIZE, LAST), 1) == 8 * iota((SIZE, LAST), 0) + 4)
    eye128 = onehot(iota((128, 128), 0) == iota((128, 128), 1))

    def slot_maps(rows):
        s = iota((1, rows), 1)
        if rows == ROWS1:
            peer = (s & (MAIN - 1)) >> 3
            rank = jnp.where(s < MAIN, s & 7, jnp.where((s & 7) < 4, 8, NEVER))
        else:
            peer = jnp.where(s < MAIN, s >> 3, (s - MAIN) >> 2)
            rank = jnp.where(s < MAIN, s & 7, 8 + (s & 3))
        spread = onehot(peer == iota((SIZE, rows), 0))
        eye = onehot(iota((rows, rows), 0) == iota((rows, rows), 1))
        return spread, rank, eye

    maps1 = slot_maps(ROWS1)
    maps2 = slot_maps(ROWS2)

    def receivers(mine_t, maps, base, g, r, rt):
        spread, rank, eye = maps
        lines = mm(mine_t, spread)
        lane = iota(lines.shape, 0)
        row = jnp.sum(jnp.where(lane == rank + base, lines, 0.0), axis=0, keepdims=True)
        flag = onehot(row.astype(I32) == lane + 1)
        rt[g] = flag
        r[g] = mm_nt(eye, flag).astype(BF)

    def send_enc(g, carry):
        rows = mm(a1[g], rows1[...])
        label = mm(mark, tm[pl.ds(pl.multiple_of(g * SIZE, SIZE), SIZE), :])
        pack_main(send1, g, rows[:MAIN])
        last = fold(rows[MAIN:]) + label
        last1[pl.ds(g * SIZE, SIZE)] = last.reshape(SIZE, 8, 128).astype(BF)
        send_group(
            g,
            0,
            ((last1, rlast1, lsem.at[0], lsem.at[2 + g]), (send1, recv1, ssem.at[0], rsem.at[0, g])),
            1,
        )
        return carry

    lax.fori_loop(0, GROUPS, send_enc, 0)

    for n in (9,):
        loads[n].wait()
    edges2 = j2.shape[1]
    q2 = onehot(iota((mesh_ref.shape[0], edges2), 0) == ms[...].reshape(1, -1))
    inside2 = jnp.where(k2 < 8, (j2 & 15) * 8 + k2, MAIN + (j2 & 15) * 4 + k2 - 8)
    place2 = (j2 >> 4) * ROWS2 + inside2
    for g in range(GROUPS):
        p = onehot(iota((ROWS2, edges2), 0) + g * ROWS2 == place2)
        a2[g] = mm_nt(p, q2).astype(BF)
        a2t[g] = mm_nt(q2, p).astype(BF)

    total[...] = jnp.zeros_like(total)

    def take_enc(g, carry):
        wait_group(g, rlast1, lsem.at[2 + g])
        last = rlast1[pl.ds(g * SIZE, SIZE)].astype(F32).reshape(LAST, 128)
        mine = mm(unmark, last.astype(BF)).astype(BF)
        mine_t = mm_nt(eye128, mine).astype(BF)
        receivers(mine_t, maps1, 0, g, r1, r1t)
        receivers(mine_t, maps2, 16, g, r2, r2t)
        picked = mm(r1[g], gathered[...])
        value_l, slope = gated(last + fold(picked[MAIN:]))
        d1l[g] = slope.astype(BF)
        wait_group(g, recv1, rsem.at[0, g])
        value, slope = gated(unpack_main(recv1, g) + picked[:MAIN])
        d1[g] = slope.astype(BF)
        both = jnp.concatenate([value.astype(BF), unfold(value_l).astype(BF)], axis=0)
        total[...] += mm(r1t[g], both)
        return carry

    lax.fori_loop(0, GROUPS, take_enc, 0)

    for n in (4, 5, 12):
        loads[n].wait()
    enc_sum = total[...]
    enc_norm, enc_scale = norm_forward(enc_sum)
    hidden = mesh_ref[...].astype(F32) + mm(enc_norm.astype(BF), w_node[...])
    hidden_ref[...] = hidden
    hidden_bf = hidden.astype(BF)
    rows1[pl.ds(0, 128), :] = mm(hidden_bf, w_send[...]).astype(BF)

    def send_msh(g, carry):
        pack(send2, g, mm(a2[g], rows1[pl.ds(0, 128), :]))
        send_group(g, 1, ((send2, recv2, ssem.at[1], rsem.at[1, g]),), 1)
        return carry

    lax.fori_loop(0, GROUPS, send_msh, 0)
    gathered[...] = mm(hidden_bf, w_recv[...]).astype(BF)
    cot_bf = cot[...]
    grad_norm = mm_nt(cot_bf, w_node[...]).astype(BF).astype(F32)
    total[...] = jnp.zeros_like(total)

    def take_msh(g, carry):
        picked = mm(r2[g], gathered[...])
        wait_group(g, recv2, rsem.at[1, g])
        value, slope = gated(unpack(recv2, g) + picked)
        d2[g] = slope.astype(BF)
        total[...] += mm(r2t[g], value.astype(BF))
        return carry

    lax.fori_loop(0, GROUPS, take_msh, 0)

    msh_sum = total[...]
    msh_norm, msh_scale = norm_forward(msh_sum)
    gathered[...] = norm_backward(grad_norm, msh_sum, msh_scale).astype(BF)

    def back_msh(g, carry):
        grad = mm(r2[g], gathered[...]) * d2[g].astype(F32)
        pack(back2, g, grad)
        send_group(g, 2, ((back2, ret2, ssem.at[2], rsem.at[2, g]),), -1)
        d2[g] = grad.astype(BF)
        return carry

    lax.fori_loop(0, GROUPS, back_msh, 0)
    out_ref[...] = (hidden_ref[...] + mm(msh_norm.astype(BF), w_node[...])).astype(BF)
    total[...] = jnp.zeros_like(total)

    def sum_msh(g, carry):
        total[...] += mm(r2t[g], d2[g])
        return carry

    lax.fori_loop(0, GROUPS, sum_msh, 0)
    part = mm_nt(total[...].astype(BF), w_recv[...])
    total[...] = jnp.zeros_like(total)

    def take_back_msh(g, carry):
        wait_group(g, ret2, rsem.at[2, g])
        total[...] += mm(a2t[g], unpack(ret2, g).astype(BF))
        return carry

    lax.fori_loop(0, GROUPS, take_back_msh, 0)
    grad_hidden_bf = (part + mm_nt(total[...].astype(BF), w_send[...])).astype(BF)
    grad_hidden = (cot_bf.astype(F32) + grad_hidden_bf.astype(F32)).astype(BF)
    grad_norm1 = mm_nt(grad_hidden, w_node[...]).astype(BF).astype(F32)
    gathered[...] = norm_backward(grad_norm1, enc_sum, enc_scale).astype(BF)

    def back_enc(g, carry):
        picked = mm(r1[g], gathered[...])
        grad = picked[:MAIN] * d1[g].astype(F32)
        grad_l = fold(picked[MAIN:]) * d1l[g].astype(F32)
        pack_main(back1, g, grad)
        blast1[pl.ds(g * SIZE, SIZE)] = grad_l.reshape(SIZE, 8, 128)[:, :4].astype(BF)
        send_group(
            g,
            3,
            ((blast1, tlast1, lsem.at[1], lsem.at[10 + g]), (back1, ret1, ssem.at[3], rsem.at[3, g])),
            -1,
        )
        d1[g] = grad.astype(BF)
        d1l[g] = grad_l.astype(BF)
        return carry

    lax.fori_loop(0, GROUPS, back_enc, 0)
    total[...] = jnp.zeros_like(total)

    def sum_enc(g, carry):
        both = jnp.concatenate([d1[g], unfold(d1l[g].astype(F32)).astype(BF)], axis=0)
        total[...] += mm(r1t[g], both)
        return carry

    lax.fori_loop(0, GROUPS, sum_enc, 0)
    mesh_part = mm_nt(total[...].astype(BF), w_recv[...]).astype(BF)
    mesh_grad[...] = (grad_hidden.astype(F32) + mesh_part.astype(F32)).astype(BF)

    def take_back_enc(g, carry):
        wait_group(g, tlast1, lsem.at[10 + g])
        half = tlast1[pl.ds(g * SIZE, SIZE)].astype(F32)
        last = jnp.concatenate([half, jnp.zeros_like(half)], axis=1).reshape(LAST, 128)
        wait_group(g, ret1, rsem.at[3, g])
        both = jnp.concatenate([unpack_main(ret1, g).astype(BF), unfold(last).astype(BF)], axis=0)
        return carry + mm(a1t[g], both)

    grid_rows = lax.fori_loop(0, GROUPS, take_back_enc, jnp.zeros(grid_ref.shape, F32))
    grid_grad[...] = mm_nt(grid_rows.astype(BF), w_grid[...]).astype(BF)

    for src, sem in (
        (send1, ssem.at[0]),
        (send2, ssem.at[1]),
        (back2, ssem.at[2]),
        (back1, ssem.at[3]),
        (last1, lsem.at[0]),
        (blast1, lsem.at[1]),
    ):
        at = src.at[pl.ds(1, PEERS - 1)]
        pltpu.make_async_copy(at, at, sem).wait()


def body(*args):
    grid_latent, mesh_latent = args[:2]
    args = [v.reshape(1, -1) if n in (7, 10) else v for n, v in enumerate(args)]
    vmem = pl.BlockSpec(memory_space=pltpu.VMEM)
    anywhere = pl.BlockSpec(memory_space=pl.ANY)
    nodes, width = mesh_latent.shape
    grid_nodes = grid_latent.shape[0]

    def block(*shape):
        return pltpu.VMEM(shape, BF)

    scratch = [pltpu.VMEM(v.shape, v.dtype) for v in args]
    scratch += [
        block(PEERS, 32, 128),
        block(PEERS, 8, 128),
        block(PEERS, 32, 128),
        block(PEERS, 8, 128),
        block(PEERS, 48, 128),
        block(PEERS, 48, 128),
        block(PEERS, 48, 128),
        block(PEERS, 48, 128),
        block(PEERS, 32, 128),
        block(PEERS, 4, 128),
        block(PEERS, 32, 128),
        block(PEERS, 4, 128),
        block(GROUPS, ROWS1, grid_nodes),
        block(GROUPS, grid_nodes, ROWS1),
        block(GROUPS, ROWS2, nodes),
        block(GROUPS, nodes, ROWS2),
        block(GROUPS, ROWS1, nodes),
        block(GROUPS, nodes, ROWS1),
        block(GROUPS, ROWS2, nodes),
        block(GROUPS, nodes, ROWS2),
        block(GROUPS, MAIN, width),
        block(GROUPS, LAST, 128),
        block(GROUPS, ROWS2, width),
        block(PEERS, 128),
        block(grid_nodes, width),
        block(nodes, width),
        pltpu.VMEM((nodes, width), F32),
        pltpu.VMEM((nodes, width), F32),
        pltpu.SemaphoreType.DMA((13,)),
        pltpu.SemaphoreType.DMA((4,)),
        pltpu.SemaphoreType.DMA((4, GROUPS)),
        pltpu.SemaphoreType.DMA((2 + 2 * GROUPS,)),
        pltpu.SemaphoreType.REGULAR,
        pltpu.SemaphoreType.REGULAR,
    ]
    return pl.pallas_call(
        kernel,
        out_shape=(
            jax.ShapeDtypeStruct(mesh_latent.shape, BF),
            jax.ShapeDtypeStruct(grid_latent.shape, BF),
            jax.ShapeDtypeStruct(mesh_latent.shape, BF),
        ),
        in_specs=[anywhere] * 13,
        out_specs=[vmem] * 3,
        scratch_shapes=scratch,
        compiler_params=pltpu.CompilerParams(
            collective_id=0, has_side_effects=True, vmem_limit_bytes=56 << 20
        ),
    )(*args)


def solution(mesh):
    rows = P(("gx", "gy"), None)
    flat = P(("gx", "gy"))
    placed = (rows, rows, P(), P(), P(), P(), flat, rows, flat, flat, rows, flat, rows)
    return jax.shard_map(
        body, mesh=mesh, in_specs=placed, out_specs=(rows, rows, rows), check_vma=False
    )
```

time: 114 us -> 98.1 us (0.86)
  Pallas kernels: 108 us -> 94 us
  local copies, waits for them, and re-layouts: 5.19 us -> 3.27 us
    pallas_call x1, Pallas kernels: 108 us -> 94 us  [body(): pl.pallas_call(kernel, out_shape=(jax.ShapeDtypeStruct(mesh_latent.shape,...]
    unnamed x11 -> x7, local copies, waits for them, and re-layouts: 4.06 us -> 3.27 us
where the time goes in v1:
time: 98.1 us; the launch traced here: 97.9 us
  Pallas kernels  94 us (96%)
  local copies, waits for them, and re-layouts  3.27 us (3%)
    pallas_call x1, Pallas kernels, body(): pl.pallas_call(kernel, out_shape=(jax.ShapeDtypeStruct(mesh_latent.shape,...  94 us
    unnamed x7, local copies, waits for them, and re-layouts  3.27 us

profile of v1, /device:TPU:1, one launch (start us, length us, event | category | flops | bytes accessed | tf_op | source)
XLA Modules:
  0.0 97.9 jit_solution(12047253073916769807)
XLA Ops:
  0.6 94.0 %shard_map.148 = (bf16[128,512]{1,0:T(8,128)(2,1)}, bf16[256,512]{1,0:T(8,128)(2,1)}, bf16[128,512]{1,0:T(8,128)(2,1)}) custom-call(bf16[256,512]{1,0:T(8,128)(2,1)} %refs_0_.1, bf16[128,512]{1,0:T(8,128)(2,1)} %refs_1_.1, bf16[512,512]{1,0:T(8,128)(2,1)} %refs_2_.1, bf16[512,512]{1,0:T(8,128)(2,1)} %refs_3_.1, bf16[512,512]{1,0:T(8,128)(2,1)} %refs_4_.1, ...), custom_call_target="tpu_custom_call" | custom-call | tf_op jit(solution)/shard_map/pallas_call | solution.py:477
  94.6 0.0 copy-start
  94.6 1.6 %copy.19 = bf16[128,512]{1,0:T(8,128)(2,1)} copy(bf16[128,512]{1,0:T(8,128)(2,1)} %get-tuple-element.6) | data formatting | bytes 262144
  96.3 0.0 copy-done
  96.3 0.0 copy-start.1
  96.3 0.7 copy.20
  97.0 0.3 copy-done.1
  97.3 0.7 copy.21
Async XLA Ops:
  94.6 1.6 %copy-start = (bf16[256,512]{1,0:T(8,128)(2,1)S(1)}, bf16[256,512]{1,0:T(8,128)(2,1)}, u32[]{:S(2)}) copy-start(bf16[256,512]{1,0:T(8,128)(2,1)} %get-tuple-element.7) | copy-start | bytes 786436
  96.3 1.0 %copy-start.1 = (bf16[128,512]{1,0:T(8,128)(2,1)S(1)}, bf16[128,512]{1,0:T(8,128)(2,1)}, u32[]{:S(2)}) copy-start(bf16[128,512]{1,0:T(8,128)(2,1)} %get-tuple-element.8) | copy-start | bytes 393220

commit v2 on v1

--- a/solution.py
+++ b/solution.py
@@ -19,6 +19,7 @@
 ROWS1 = MAIN + LAST
 ROWS2 = MAIN + TAIL
 NEVER = 99
+NEAR_LAST = sorted(range(SIZE), key=lambda k: -min(k // 4, 4 - k // 4) - min(k % 4, 4 - k % 4))
 
 
 def coords():
@@ -65,6 +66,29 @@
     b = wire[at, 16:32, :].astype(F32)
     parts = (a[:, :8], a[:, 8:], b[:, :8], b[:, 8:])
     return jnp.concatenate([v.reshape(MAIN, 128) for v in parts], axis=1)
+
+
+def pack_units(wire, g, rows, last):
+    at = pl.ds(g * SIZE, SIZE)
+    for q in range(4):
+        m = quarter(rows, q).reshape(SIZE, 8, 128)
+        wire[at, 2 * q] = m[:, :4].astype(BF)
+        wire[at, 2 * q + 1] = m[:, 4:].astype(BF)
+    last = last.reshape(SIZE, 8, 128)
+    wire[at, 8] = last[:, :4].astype(BF)
+    if wire.shape[1] > 9:
+        wire[at, 9] = last[:, 4:].astype(BF)
+
+
+def unpack_units(wire, g):
+    at = pl.ds(g * SIZE, SIZE)
+
+    def pair(n):
+        low = wire[at, n].astype(F32)
+        high = wire[at, n + 1].astype(F32) if n + 1 < wire.shape[1] else jnp.zeros_like(low)
+        return jnp.concatenate([low, high], axis=1).reshape(MAIN, 128)
+
+    return jnp.concatenate([pair(2 * q) for q in range(4)], axis=1), pair(8)
 
 
 def pack_tail(wire, g, rows):
@@ -127,14 +151,13 @@
     local, refs = refs[:13], refs[13:]
     grid_ref, mesh_ref, w_grid, w_recv, w_send, w_node, es, eo, et, ms, mo, mt, cot = local
     (
-        send1, last1, recv1, rlast1, send2, recv2, back2, ret2, back1, blast1, ret1, tlast1,
+        send1, recv1, send2, recv2, back2, ret2, back1, ret1,
         a1, a1t, a2, a2t, r1, r1t, r2, r2t, d1, d1l, d2,
         tm, rows1, gathered, total, hidden_ref,
-        isem, ssem, rsem, lsem, zsem, ysem,
+        isem, ssem, rsem, psem,
     ) = refs
 
     y, z, x, c = coords()
-    gy = z * 8 + x * 2 + c
 
     loads = [pltpu.make_async_copy(a, b, isem.at[n]) for n, (a, b) in enumerate(zip(inputs, local))]
     order = (7, 10, 8, 11, 6, 9, 0, 2, 1, 3, 5, 4, 12)
@@ -142,15 +165,14 @@
         loads[n].start()
 
     barrier = pltpu.get_barrier_semaphore()
-    ring_x = [(y, z * 8 + ((x + d // 2) % 4) * 2 + (c + d) % 2) for d in range(1, 8)]
-    ring_z = [(y, ((z + d) % 4) * 8 + x * 2 + c) for d in range(1, 4)]
-    ring_y = [((y + d) % 4, gy) for d in range(1, 4)]
+    ring = [(y, z * 8 + ((x + d // 2) % 4) * 2 + (c + d) % 2) for d in range(1, 8)]
+    plane = [((y + d // 4) % 4, ((z + d) % 4) * 8 + x * 2 + c) for d in range(1, 16)]
 
     def greet(sem, ring):
         for device in ring:
             pl.semaphore_signal(sem, inc=1, device_id=device, device_id_type=MESH)
 
-    greet(barrier, ring_x + ring_z + ring_y)
+    greet(barrier, ring + plane)
 
     def route(owner):
         edges = owner.shape[1]
@@ -177,8 +199,8 @@
         mm_nt(same1, labels(k1, et[...].reshape(1, -1), 0)) + mm_nt(same2, labels(k2, mt[...].reshape(1, -1), 16))
     ).astype(BF)
 
-    pl.semaphore_wait(barrier, 13)
-    greet(zsem, ring_z)
+    pl.semaphore_wait(barrier, 22)
+    greet(psem, plane)
 
     loads[6].wait()
     edges1 = j1.shape[1]
@@ -193,9 +215,6 @@
         a1[g] = mm_nt(p, q1).astype(BF)
         a1t[g] = mm_nt(q1, p).astype(BF)
 
-    pl.semaphore_wait(zsem, 3)
-    greet(ysem, ring_y)
-
     for n in (0, 2):
         loads[n].wait()
     rows1[...] = mm(grid_ref[...], w_grid[...]).astype(BF)
@@ -203,27 +222,25 @@
         loads[n].wait()
     gathered[...] = mm(mesh_ref[...], w_recv[...]).astype(BF)
 
-    pl.semaphore_wait(ysem, 3)
-
-    def send_group(g, phase, wires, sign):
+    pl.semaphore_wait(psem, 15)
+
+    def send_group(g, src, dst, s, r, sign):
         gh, gl = g // 2, g % 2
         tc = (c + gl) % 2
         ty = [(y + sign * (gh + m) + 8) % 4 for m in range(4)]
-        for k in range(SIZE):
+        for k in NEAR_LAST:
             kz, kx = k // 4, k % 4
             tz, tx = (z + sign * kz + 4) % 4, (x + sign * kx + 4) % 4
             device = (ty[(kz + kx) % 4], tz * 8 + tx * 2 + tc)
             j = g * SIZE + k
 
             def remote():
-                for src, dst, s, r in wires:
-                    pltpu.make_async_remote_copy(
-                        src.at[j], dst.at[j], s, r, device_id=device, device_id_type=MESH
-                    ).start()
+                pltpu.make_async_remote_copy(
+                    src.at[j], dst.at[j], s, r, device_id=device, device_id_type=MESH
+                ).start()
 
             def mine():
-                for src, dst, s, r in wires:
-                    pltpu.make_async_copy(src.at[j], dst.at[j], r).start()
+                pltpu.make_async_copy(src.at[j], dst.at[j], r).start()
 
             if k == 0:
                 pl.when(g > 0)(remote)
@@ -266,15 +283,8 @@
     def send_enc(g, carry):
         rows = mm(a1[g], rows1[...])
         label = mm(mark, tm[pl.ds(pl.multiple_of(g * SIZE, SIZE), SIZE), :])
-        pack_main(send1, g, rows[:MAIN])
-        last = fold(rows[MAIN:]) + label
-        last1[pl.ds(g * SIZE, SIZE)] = last.reshape(SIZE, 8, 128).astype(BF)
-        send_group(
-            g,
-            0,
-            ((last1, rlast1, lsem.at[0], lsem.at[2 + g]), (send1, recv1, ssem.at[0], rsem.at[0, g])),
-            1,
-        )
+        pack_units(send1, g, rows[:MAIN], fold(rows[MAIN:]) + label)
+        send_group(g, send1, recv1, ssem.at[0], rsem.at[0, g], 1)
         return carry
 
     lax.fori_loop(0, GROUPS, send_enc, 0)
@@ -293,8 +303,8 @@
     total[...] = jnp.zeros_like(total)
 
     def take_enc(g, carry):
-        wait_group(g, rlast1, lsem.at[2 + g])
-        last = rlast1[pl.ds(g * SIZE, SIZE)].astype(F32).reshape(LAST, 128)
+        wait_group(g, recv1, rsem.at[0, g])
+        rows, last = unpack_units(recv1, g)
         mine = mm(unmark, last.astype(BF)).astype(BF)
         mine_t = mm_nt(eye128, mine).astype(BF)
         receivers(mine_t, maps1, 0, g, r1, r1t)
@@ -302,8 +312,7 @@
         picked = mm(r1[g], gathered[...])
         value_l, slope = gated(last + fold(picked[MAIN:]))
         d1l[g] = slope.astype(BF)
-        wait_group(g, recv1, rsem.at[0, g])
-        value, slope = gated(unpack_main(recv1, g) + picked[:MAIN])
+        value, slope = gated(rows + picked[:MAIN])
         d1[g] = slope.astype(BF)
         both = jnp.concatenate([value.astype(BF), unfold(value_l).astype(BF)], axis=0)
         total[...] += mm(r1t[g], both)
@@ -322,7 +331,7 @@
 
     def send_msh(g, carry):
         pack(send2, g, mm(a2[g], rows1[pl.ds(0, 128), :]))
-        send_group(g, 1, ((send2, recv2, ssem.at[1], rsem.at[1, g]),), 1)
+        send_group(g, send2, recv2, ssem.at[1], rsem.at[1, g], 1)
         return carry
 
     lax.fori_loop(0, GROUPS, send_msh, 0)
@@ -348,7 +357,7 @@
     def back_msh(g, carry):
         grad = mm(r2[g], gathered[...]) * d2[g].astype(F32)
         pack(back2, g, grad)
-        send_group(g, 2, ((back2, ret2, ssem.at[2], rsem.at[2, g]),), -1)
+        send_group(g, back2, ret2, ssem.at[2], rsem.at[2, g], -1)
         d2[g] = grad.astype(BF)
         return carry
 
@@ -379,14 +388,8 @@
         picked = mm(r1[g], gathered[...])
         grad = picked[:MAIN] * d1[g].astype(F32)
         grad_l = fold(picked[MAIN:]) * d1l[g].astype(F32)
-        pack_main(back1, g, grad)
-        blast1[pl.ds(g * SIZE, SIZE)] = grad_l.reshape(SIZE, 8, 128)[:, :4].astype(BF)
-        send_group(
-            g,
-            3,
-            ((blast1, tlast1, lsem.at[1], lsem.at[10 + g]), (back1, ret1, ssem.at[3], rsem.at[3, g])),
-            -1,
-        )
+        pack_units(back1, g, grad, grad_l)
+        send_group(g, back1, ret1, ssem.at[3], rsem.at[3, g], -1)
         d1[g] = grad.astype(BF)
         d1l[g] = grad_l.astype(BF)
         return carry
@@ -404,11 +407,9 @@
     mesh_grad[...] = (grad_hidden.astype(F32) + mesh_part.astype(F32)).astype(BF)
 
     def take_back_enc(g, carry):
-        wait_group(g, tlast1, lsem.at[10 + g])
-        half = tlast1[pl.ds(g * SIZE, SIZE)].astype(F32)
-        last = jnp.concatenate([half, jnp.zeros_like(half)], axis=1).reshape(LAST, 128)
         wait_group(g, ret1, rsem.at[3, g])
-        both = jnp.concatenate([unpack_main(ret1, g).astype(BF), unfold(last).astype(BF)], axis=0)
+        rows, last = unpack_units(ret1, g)
+        both = jnp.concatenate([rows.astype(BF), unfold(last).astype(BF)], axis=0)
         return carry + mm(a1t[g], both)
 
     grid_rows = lax.fori_loop(0, GROUPS, take_back_enc, jnp.zeros(grid_ref.shape, F32))
@@ -419,11 +420,14 @@
         (send2, ssem.at[1]),
         (back2, ssem.at[2]),
         (back1, ssem.at[3]),
-        (last1, lsem.at[0]),
-        (blast1, lsem.at[1]),
     ):
         at = src.at[pl.ds(1, PEERS - 1)]
         pltpu.make_async_copy(at, at, sem).wait()
+
+
+def hand_on(*refs):
+    for n in range(3):
+        refs[n + 3][...] = refs[n][...]
 
 
 def body(*args):
@@ -439,18 +443,14 @@
 
     scratch = [pltpu.VMEM(v.shape, v.dtype) for v in args]
     scratch += [
-        block(PEERS, 32, 128),
-        block(PEERS, 8, 128),
-        block(PEERS, 32, 128),
-        block(PEERS, 8, 128),
+        block(PEERS, 10, 4, 128),
+        block(PEERS, 10, 4, 128),
         block(PEERS, 48, 128),
         block(PEERS, 48, 128),
         block(PEERS, 48, 128),
         block(PEERS, 48, 128),
-        block(PEERS, 32, 128),
-        block(PEERS, 4, 128),
-        block(PEERS, 32, 128),
-        block(PEERS, 4, 128),
+        block(PEERS, 9, 4, 128),
+        block(PEERS, 9, 4, 128),
         block(GROUPS, ROWS1, grid_nodes),
         block(GROUPS, grid_nodes, ROWS1),
         block(GROUPS, ROWS2, nodes),
@@ -470,11 +470,9 @@
         pltpu.SemaphoreType.DMA((13,)),
         pltpu.SemaphoreType.DMA((4,)),
         pltpu.SemaphoreType.DMA((4, GROUPS)),
-        pltpu.SemaphoreType.DMA((2 + 2 * GROUPS,)),
-        pltpu.SemaphoreType.REGULAR,
         pltpu.SemaphoreType.REGULAR,
     ]
-    return pl.pallas_call(
+    results = pl.pallas_call(
         kernel,
         out_shape=(
             jax.ShapeDtypeStruct(mesh_latent.shape, BF),
@@ -488,6 +486,12 @@
             collective_id=0, has_side_effects=True, vmem_limit_bytes=56 << 20
         ),
     )(*args)
+    return pl.pallas_call(
+        hand_on,
+        out_shape=[jax.ShapeDtypeStruct(v.shape, v.dtype) for v in results],
+        in_specs=[vmem] * 3,
+        out_specs=[vmem] * 3,
+    )(*results)
 
 
 def solution(mesh):

time: 98.1 us -> 95.6 us (0.975)
  local copies, waits for them, and re-layouts: 3.27 us -> 0 us
    unnamed x7 -> x0, local copies, waits for them, and re-layouts: 3.27 us -> none
    pallas_call x0 -> x1, Pallas kernels: none -> 1.85 us  [body(): pl.pallas_call(hand_on, out_shape=[jax.ShapeDtypeStruct(v.shape, v.dtype)...]
    pallas_call x1, Pallas kernels: 94 us -> 92.9 us  [body(): pl.pallas_call(kernel, out_shape=(jax.ShapeDtypeStruct(mesh_latent.shape,...]
where the time goes in v2:
time: 95.6 us; the launch traced here: 95.4 us
  Pallas kernels  94.8 us (99%)
    pallas_call x1, Pallas kernels, body(): pl.pallas_call(kernel, out_shape=(jax.ShapeDtypeStruct(mesh_latent.shape,...  92.9 us

profile of v2, /device:TPU:1, one launch (start us, length us, event | category | flops | bytes accessed | tf_op | source)
XLA Modules:
  0.0 95.4 jit_solution(5808329687460934889)
XLA Ops:
  0.6 92.9 %shard_map.148 = (bf16[128,512]{1,0:T(8,128)(2,1)}, bf16[256,512]{1,0:T(8,128)(2,1)}, bf16[128,512]{1,0:T(8,128)(2,1)}) custom-call(bf16[256,512]{1,0:T(8,128)(2,1)} %refs_0_.1, bf16[128,512]{1,0:T(8,128)(2,1)} %refs_1_.1, bf16[512,512]{1,0:T(8,128)(2,1)} %refs_2_.1, bf16[512,512]{1,0:T(8,128)(2,1)} %refs_3_.1, bf16[512,512]{1,0:T(8,128)(2,1)} %refs_4_.1, ...), custom_call_target="tpu_custom_call" | custom-call | tf_op jit(solution)/shard_map/pallas_call | solution.py:475
  93.6 1.9 %shard_map.149 = (bf16[128,512]{1,0:T(8,128)(2,1)}, bf16[256,512]{1,0:T(8,128)(2,1)}, bf16[128,512]{1,0:T(8,128)(2,1)}) custom-call(bf16[128,512]{1,0:T(8,128)(2,1)} %get-tuple-element.6.refs_0_, bf16[256,512]{1,0:T(8,128)(2,1)} %get-tuple-element.7.refs_1_, bf16[128,512]{1,0:T(8,128)(2,1)} %get-tuple-element.8.refs_2_), custom_call_target="tpu_custom_call" | custom-call | tf_op jit(solution)/shard_map/pallas_call | solution.py:489

commit v3 on v2

--- a/solution.py
+++ b/solution.py
@@ -76,8 +76,6 @@
         wire[at, 2 * q + 1] = m[:, 4:].astype(BF)
     last = last.reshape(SIZE, 8, 128)
     wire[at, 8] = last[:, :4].astype(BF)
-    if wire.shape[1] > 9:
-        wire[at, 9] = last[:, 4:].astype(BF)
 
 
 def unpack_units(wire, g):
@@ -153,8 +151,8 @@
     (
         send1, recv1, send2, recv2, back2, ret2, back1, ret1,
         a1, a1t, a2, a2t, r1, r1t, r2, r2t, d1, d1l, d2,
-        tm, rows1, gathered, total, hidden_ref,
-        isem, ssem, rsem, psem,
+        told, ring_told, plane_told, heard, rows1, gathered, total, hidden_ref,
+        isem, ssem, rsem, rlsem, plsem, psem,
     ) = refs
 
     y, z, x, c = coords()
@@ -181,7 +179,7 @@
         dx = (((owner >> 1) & 3) - x) & 3
         dc = ((owner & 1) - c) & 1
         j = (((dy - dz - dx) & 3) * 2 + dc) * SIZE + dz * 4 + dx
-        same = iota((PEERS, edges), 0) == j
+        same = iota((PEERS, edges), 0) == (dx * 2 + dc) * 16 + dy * 4 + dz
         before = onehot(iota((edges, edges), 0) < iota((edges, edges), 1))
         count = mm(onehot(same), before)
         rank = jnp.sum(jnp.where(same, count, 0.0), axis=0, keepdims=True).astype(I32)
@@ -195,12 +193,21 @@
         loads[n].wait()
     j1, k1, same1 = route(eo[...])
     j2, k2, same2 = route(mo[...])
-    tm[...] = (
+    told[...] = (
         mm_nt(same1, labels(k1, et[...].reshape(1, -1), 0)) + mm_nt(same2, labels(k2, mt[...].reshape(1, -1), 16))
-    ).astype(BF)
+    ).astype(BF).reshape(8, 16, 128)
 
     pl.semaphore_wait(barrier, 22)
     greet(psem, plane)
+
+    def pass_on(src, dst, sem, devices):
+        pltpu.make_async_copy(src.at[0], dst.at[0], sem.at[1]).start()
+        for n, device in enumerate(devices):
+            pltpu.make_async_remote_copy(
+                src.at[n + 1], dst.at[n + 1], sem.at[0], sem.at[1], device_id=device, device_id_type=MESH
+            ).start()
+
+    pass_on(told, ring_told, rlsem, ring)
 
     loads[6].wait()
     edges1 = j1.shape[1]
@@ -252,8 +259,6 @@
         at = dst.at[pl.ds(g * SIZE, SIZE)]
         pltpu.make_async_copy(at, at, sem).wait()
 
-    mark = onehot(iota((LAST, SIZE), 0) == 8 * iota((LAST, SIZE), 1) + 4)
-    unmark = onehot(iota((SIZE, LAST), 1) == 8 * iota((SIZE, LAST), 0) + 4)
     eye128 = onehot(iota((128, 128), 0) == iota((128, 128), 1))
 
     def slot_maps(rows):
@@ -264,16 +269,15 @@
         else:
             peer = jnp.where(s < MAIN, s >> 3, (s - MAIN) >> 2)
             rank = jnp.where(s < MAIN, s & 7, 8 + (s & 3))
-        spread = onehot(peer == iota((SIZE, rows), 0))
         eye = onehot(iota((rows, rows), 0) == iota((rows, rows), 1))
-        return spread, rank, eye
+        return peer, rank, eye
 
     maps1 = slot_maps(ROWS1)
     maps2 = slot_maps(ROWS2)
 
     def receivers(mine_t, maps, base, g, r, rt):
-        spread, rank, eye = maps
-        lines = mm(mine_t, spread)
+        peer, rank, eye = maps
+        lines = mm(mine_t, onehot(iota((PEERS, rank.shape[1]), 0) == peer + g * SIZE))
         lane = iota(lines.shape, 0)
         row = jnp.sum(jnp.where(lane == rank + base, lines, 0.0), axis=0, keepdims=True)
         flag = onehot(row.astype(I32) == lane + 1)
@@ -282,12 +286,19 @@
 
     def send_enc(g, carry):
         rows = mm(a1[g], rows1[...])
-        label = mm(mark, tm[pl.ds(pl.multiple_of(g * SIZE, SIZE), SIZE), :])
-        pack_units(send1, g, rows[:MAIN], fold(rows[MAIN:]) + label)
+        pack_units(send1, g, rows[:MAIN], fold(rows[MAIN:]))
         send_group(g, send1, recv1, ssem.at[0], rsem.at[0, g], 1)
         return carry
 
-    lax.fori_loop(0, GROUPS, send_enc, 0)
+    send_enc(0, 0)
+
+    pltpu.make_async_copy(ring_told, ring_told, rlsem.at[1]).wait()
+    line = iota((PEERS, PEERS), 0)
+    turn = onehot(iota((PEERS, PEERS), 1) == (line & 7) * 16 + (line >> 3))
+    plane_told[...] = mm(turn, ring_told[...].reshape(PEERS, 128)).reshape(16, 8, 128).astype(BF)
+    pass_on(plane_told, heard, plsem, plane)
+
+    lax.fori_loop(1, GROUPS, send_enc, 0)
 
     for n in (9,):
         loads[n].wait()
@@ -302,14 +313,20 @@
 
     total[...] = jnp.zeros_like(total)
 
+    pltpu.make_async_copy(heard, heard, plsem.at[1]).wait()
+    zx, gc = line & 15, line >> 4
+    n_dy = ((gc >> 1) + (zx >> 2) + zx) & 3
+    at = (n_dy * 4 + (zx >> 2)) * 8 + (zx & 3) * 2 + (gc & 1)
+    order = onehot(iota((PEERS, PEERS), 1) == at)
+    mine = mm(order, heard[...].astype(F32).reshape(PEERS, 128).astype(BF)).astype(BF)
+    mine_t = mm_nt(eye128, mine).astype(BF)
+
     def take_enc(g, carry):
-        wait_group(g, recv1, rsem.at[0, g])
-        rows, last = unpack_units(recv1, g)
-        mine = mm(unmark, last.astype(BF)).astype(BF)
-        mine_t = mm_nt(eye128, mine).astype(BF)
         receivers(mine_t, maps1, 0, g, r1, r1t)
         receivers(mine_t, maps2, 16, g, r2, r2t)
         picked = mm(r1[g], gathered[...])
+        wait_group(g, recv1, rsem.at[0, g])
+        rows, last = unpack_units(recv1, g)
         value_l, slope = gated(last + fold(picked[MAIN:]))
         d1l[g] = slope.astype(BF)
         value, slope = gated(rows + picked[:MAIN])
@@ -420,8 +437,10 @@
         (send2, ssem.at[1]),
         (back2, ssem.at[2]),
         (back1, ssem.at[3]),
+        (told, rlsem.at[0]),
+        (plane_told, plsem.at[0]),
     ):
-        at = src.at[pl.ds(1, PEERS - 1)]
+        at = src.at[pl.ds(1, src.shape[0] - 1)]
         pltpu.make_async_copy(at, at, sem).wait()
 
 
@@ -443,8 +462,8 @@
 
     scratch = [pltpu.VMEM(v.shape, v.dtype) for v in args]
     scratch += [
-        block(PEERS, 10, 4, 128),
-        block(PEERS, 10, 4, 128),
+        block(PEERS, 9, 4, 128),
+        block(PEERS, 9, 4, 128),
         block(PEERS, 48, 128),
         block(PEERS, 48, 128),
         block(PEERS, 48, 128),
@@ -462,7 +481,10 @@
         block(GROUPS, MAIN, width),
         block(GROUPS, LAST, 128),
         block(GROUPS, ROWS2, width),
-        block(PEERS, 128),
+        block(8, 16, 128),
+        block(8, 16, 128),
+        block(16, 8, 128),
+        block(16, 8, 128),
         block(grid_nodes, width),
         block(nodes, width),
         pltpu.VMEM((nodes, width), F32),
@@ -470,6 +492,8 @@
         pltpu.SemaphoreType.DMA((13,)),
         pltpu.SemaphoreType.DMA((4,)),
         pltpu.SemaphoreType.DMA((4, GROUPS)),
+        pltpu.SemaphoreType.DMA((2,)),
+        pltpu.SemaphoreType.DMA((2,)),
         pltpu.SemaphoreType.REGULAR,
     ]
     results = pl.pallas_call(

time: 95.6 us -> 93.9 us (0.982)
  Pallas kernels: 94.8 us -> 93.2 us
    pallas_call x1, Pallas kernels: 92.9 us -> 91.3 us  [body(): pl.pallas_call(kernel, out_shape=(jax.ShapeDtypeStruct(mesh_latent.shape,...]
where the time goes in v3:
time: 93.9 us; the launch traced here: 93.8 us
  Pallas kernels  93.2 us (99%)
    pallas_call x1, Pallas kernels, body(): pl.pallas_call(kernel, out_shape=(jax.ShapeDtypeStruct(mesh_latent.shape,...  91.3 us

profile of v3, /device:TPU:1, one launch (start us, length us, event | category | flops | bytes accessed | tf_op | source)
XLA Modules:
  0.0 93.8 jit_solution(5254299615056841525)
XLA Ops:
  0.6 91.3 %shard_map.148 = (bf16[128,512]{1,0:T(8,128)(2,1)}, bf16[256,512]{1,0:T(8,128)(2,1)}, bf16[128,512]{1,0:T(8,128)(2,1)}) custom-call(bf16[256,512]{1,0:T(8,128)(2,1)} %refs_0_.1, bf16[128,512]{1,0:T(8,128)(2,1)} %refs_1_.1, bf16[512,512]{1,0:T(8,128)(2,1)} %refs_2_.1, bf16[512,512]{1,0:T(8,128)(2,1)} %refs_3_.1, bf16[512,512]{1,0:T(8,128)(2,1)} %refs_4_.1, ...), custom_call_target="tpu_custom_call" | custom-call | tf_op jit(solution)/shard_map/pallas_call | solution.py:499
  91.9 1.9 %shard_map.149 = (bf16[128,512]{1,0:T(8,128)(2,1)}, bf16[256,512]{1,0:T(8,128)(2,1)}, bf16[128,512]{1,0:T(8,128)(2,1)}) custom-call(bf16[128,512]{1,0:T(8,128)(2,1)} %get-tuple-element.6.refs_0_, bf16[256,512]{1,0:T(8,128)(2,1)} %get-tuple-element.7.refs_1_, bf16[128,512]{1,0:T(8,128)(2,1)} %get-tuple-element.8.refs_2_), custom_call_target="tpu_custom_call" | custom-call | tf_op jit(solution)/shard_map/pallas_call | solution.py:513

commit v4 on v3

--- a/solution.py
+++ b/solution.py
@@ -157,20 +157,23 @@
 
     y, z, x, c = coords()
 
+    barrier = pltpu.get_barrier_semaphore()
+    ring = [(y, z * 8 + ((x + d // 2) % 4) * 2 + (c + d) % 2) for d in range(1, 8)]
+    plane = [((y + d // 4) % 4, ((z + d) % 4) * 8 + x * 2 + c) for d in range(1, 16)]
+
+    def greet(sem, ring):
+        for device in ring:
+            pl.semaphore_signal(sem, inc=1, device_id=device, device_id_type=MESH)
+
+    far = sorted(range(1, 64), key=lambda i: -sum(min(d, 4 - d) for d in (i // 16, i // 4 % 4, i % 4)))
+    like = [((y + i // 16) % 4, ((z + i // 4) % 4) * 8 + ((x + i) % 4) * 2 + c) for i in far]
+    twin = [(y, z * 8 + x * 2 + 1 - c)]
+    greet(barrier, like + twin)
+
     loads = [pltpu.make_async_copy(a, b, isem.at[n]) for n, (a, b) in enumerate(zip(inputs, local))]
     order = (7, 10, 8, 11, 6, 9, 0, 2, 1, 3, 5, 4, 12)
     for n in order:
         loads[n].start()
-
-    barrier = pltpu.get_barrier_semaphore()
-    ring = [(y, z * 8 + ((x + d // 2) % 4) * 2 + (c + d) % 2) for d in range(1, 8)]
-    plane = [((y + d // 4) % 4, ((z + d) % 4) * 8 + x * 2 + c) for d in range(1, 16)]
-
-    def greet(sem, ring):
-        for device in ring:
-            pl.semaphore_signal(sem, inc=1, device_id=device, device_id_type=MESH)
-
-    greet(barrier, ring + plane)
 
     def route(owner):
         edges = owner.shape[1]
@@ -197,8 +200,30 @@
         mm_nt(same1, labels(k1, et[...].reshape(1, -1), 0)) + mm_nt(same2, labels(k2, mt[...].reshape(1, -1), 16))
     ).astype(BF).reshape(8, 16, 128)
 
-    pl.semaphore_wait(barrier, 22)
-    greet(psem, plane)
+    loads[6].wait()
+    edges1 = j1.shape[1]
+    q1 = onehot(iota((grid_ref.shape[0], edges1), 0) == es[...].reshape(1, -1))
+    main1 = jnp.where(k1 < 8, j1 * 8 + k1, -1)
+    last1_of = jnp.where(k1 == 8, j1, -1)
+    row1 = iota((MAIN, edges1), 0)
+    def places1(g):
+        p_main = onehot(row1 + g * MAIN == main1)
+        p_last = onehot(jnp.where((row1 & 7) < 4, (row1 >> 3) + g * SIZE, -2) == last1_of)
+        return jnp.concatenate([p_main, p_last], axis=0)
+
+    for g in range(GROUPS):
+        a1[g] = mm_nt(places1(g), q1).astype(BF)
+
+    for n in (0, 2):
+        loads[n].wait()
+    rows1[...] = mm(grid_ref[...], w_grid[...]).astype(BF)
+    for n in (1, 3):
+        loads[n].wait()
+    gathered[...] = mm(mesh_ref[...], w_recv[...]).astype(BF)
+
+    pl.semaphore_wait(barrier, 64)
+    greet(psem, twin)
+    pl.semaphore_wait(psem, 1)
 
     def pass_on(src, dst, sem, devices):
         pltpu.make_async_copy(src.at[0], dst.at[0], sem.at[1]).start()
@@ -208,28 +233,6 @@
             ).start()
 
     pass_on(told, ring_told, rlsem, ring)
-
-    loads[6].wait()
-    edges1 = j1.shape[1]
-    q1 = onehot(iota((grid_ref.shape[0], edges1), 0) == es[...].reshape(1, -1))
-    main1 = jnp.where(k1 < 8, j1 * 8 + k1, -1)
-    last1_of = jnp.where(k1 == 8, j1, -1)
-    row1 = iota((MAIN, edges1), 0)
-    for g in range(GROUPS):
-        p_main = onehot(row1 + g * MAIN == main1)
-        p_last = onehot(jnp.where((row1 & 7) < 4, (row1 >> 3) + g * SIZE, -2) == last1_of)
-        p = jnp.concatenate([p_main, p_last], axis=0)
-        a1[g] = mm_nt(p, q1).astype(BF)
-        a1t[g] = mm_nt(q1, p).astype(BF)
-
-    for n in (0, 2):
-        loads[n].wait()
-    rows1[...] = mm(grid_ref[...], w_grid[...]).astype(BF)
-    for n in (1, 3):
-        loads[n].wait()
-    gathered[...] = mm(mesh_ref[...], w_recv[...]).astype(BF)
-
-    pl.semaphore_wait(psem, 15)
 
     def send_group(g, src, dst, s, r, sign):
         gh, gl = g // 2, g % 2
@@ -290,7 +293,7 @@
         send_group(g, send1, recv1, ssem.at[0], rsem.at[0, g], 1)
         return carry
 
-    send_enc(0, 0)
+    lax.fori_loop(0, 2, send_enc, 0)
 
     pltpu.make_async_copy(ring_told, ring_told, rlsem.at[1]).wait()
     line = iota((PEERS, PEERS), 0)
@@ -298,8 +301,10 @@
     plane_told[...] = mm(turn, ring_told[...].reshape(PEERS, 128)).reshape(16, 8, 128).astype(BF)
     pass_on(plane_told, heard, plsem, plane)
 
-    lax.fori_loop(1, GROUPS, send_enc, 0)
-
+    lax.fori_loop(2, GROUPS, send_enc, 0)
+
+    for g in range(GROUPS):
+        a1t[g] = mm_nt(q1, places1(g)).astype(BF)
     for n in (9,):
         loads[n].wait()
     edges2 = j2.shape[1]

time: 93.9 us -> 92.9 us (0.989)
  Pallas kernels: 93.2 us -> 92.1 us
    pallas_call x1, Pallas kernels: 91.3 us -> 90.3 us  [body(): pl.pallas_call(kernel, out_shape=(jax.ShapeDtypeStruct(mesh_latent.shape,...]
where the time goes in v4:
time: 92.9 us; the launch traced here: 92.8 us
  Pallas kernels  92.1 us (99%)
    pallas_call x1, Pallas kernels, body(): pl.pallas_call(kernel, out_shape=(jax.ShapeDtypeStruct(mesh_latent.shape,...  90.3 us

profile of v4, /device:TPU:1, one launch (start us, length us, event | category | flops | bytes accessed | tf_op | source)
XLA Modules:
  0.0 92.8 jit_solution(91773624470917978)
XLA Ops:
  0.6 90.3 %shard_map.148 = (bf16[128,512]{1,0:T(8,128)(2,1)}, bf16[256,512]{1,0:T(8,128)(2,1)}, bf16[128,512]{1,0:T(8,128)(2,1)}) custom-call(bf16[256,512]{1,0:T(8,128)(2,1)} %refs_0_.1, bf16[128,512]{1,0:T(8,128)(2,1)} %refs_1_.1, bf16[512,512]{1,0:T(8,128)(2,1)} %refs_2_.1, bf16[512,512]{1,0:T(8,128)(2,1)} %refs_3_.1, bf16[512,512]{1,0:T(8,128)(2,1)} %refs_4_.1, ...), custom_call_target="tpu_custom_call" | custom-call | tf_op jit(solution)/shard_map/pallas_call | solution.py:504
  90.9 1.9 %shard_map.149 = (bf16[128,512]{1,0:T(8,128)(2,1)}, bf16[256,512]{1,0:T(8,128)(2,1)}, bf16[128,512]{1,0:T(8,128)(2,1)}) custom-call(bf16[128,512]{1,0:T(8,128)(2,1)} %get-tuple-element.6.refs_0_, bf16[256,512]{1,0:T(8,128)(2,1)} %get-tuple-element.7.refs_1_, bf16[128,512]{1,0:T(8,128)(2,1)} %get-tuple-element.8.refs_2_), custom_call_target="tpu_custom_call" | custom-call | tf_op jit(solution)/shard_map/pallas_call | solution.py:518

commit v5 on v4

--- a/solution.py
+++ b/solution.py
@@ -151,7 +151,7 @@
     (
         send1, recv1, send2, recv2, back2, ret2, back1, ret1,
         a1, a1t, a2, a2t, r1, r1t, r2, r2t, d1, d1l, d2,
-        told, ring_told, plane_told, heard, rows1, gathered, total, hidden_ref,
+        told, ring_told, plane_told, heard, rows1, gathered, total, hidden_ref, grid_sum,
         isem, ssem, rsem, rlsem, plsem, psem,
     ) = refs
 
@@ -417,6 +417,7 @@
         return carry
 
     lax.fori_loop(0, GROUPS, back_enc, 0)
+    grid_sum[...] = jnp.zeros_like(grid_sum)
     total[...] = jnp.zeros_like(total)
 
     def sum_enc(g, carry):
@@ -432,9 +433,11 @@
         wait_group(g, ret1, rsem.at[3, g])
         rows, last = unpack_units(ret1, g)
         both = jnp.concatenate([rows.astype(BF), unfold(last).astype(BF)], axis=0)
-        return carry + mm(a1t[g], both)
-
-    grid_rows = lax.fori_loop(0, GROUPS, take_back_enc, jnp.zeros(grid_ref.shape, F32))
+        grid_sum[...] += mm(a1t[g], both)
+        return carry
+
+    lax.fori_loop(0, GROUPS, take_back_enc, 0)
+    grid_rows = grid_sum[...]
     grid_grad[...] = mm_nt(grid_rows.astype(BF), w_grid[...]).astype(BF)
 
     for src, sem in (
@@ -494,6 +497,7 @@
         block(nodes, width),
         pltpu.VMEM((nodes, width), F32),
         pltpu.VMEM((nodes, width), F32),
+        pltpu.VMEM((grid_nodes, width), F32),
         pltpu.SemaphoreType.DMA((13,)),
         pltpu.SemaphoreType.DMA((4,)),
         pltpu.SemaphoreType.DMA((4, GROUPS)),

time: 92.9 us -> 92.9 us (level)
  no operation moved by 1% of the time
where the time goes in v5:
time: 92.9 us; the launch traced here: 92.7 us
  Pallas kernels  92.1 us (99%)
    pallas_call x1, Pallas kernels, body(): pl.pallas_call(kernel, out_shape=(jax.ShapeDtypeStruct(mesh_latent.shape,...  90.2 us

profile of v5, /device:TPU:1, one launch (start us, length us, event | category | flops | bytes accessed | tf_op | source)
XLA Modules:
  0.0 92.7 jit_solution(1628405573072384728)
XLA Ops:
  0.6 90.2 %shard_map.148 = (bf16[128,512]{1,0:T(8,128)(2,1)}, bf16[256,512]{1,0:T(8,128)(2,1)}, bf16[128,512]{1,0:T(8,128)(2,1)}) custom-call(bf16[256,512]{1,0:T(8,128)(2,1)} %refs_0_.1, bf16[128,512]{1,0:T(8,128)(2,1)} %refs_1_.1, bf16[512,512]{1,0:T(8,128)(2,1)} %refs_2_.1, bf16[512,512]{1,0:T(8,128)(2,1)} %refs_3_.1, bf16[512,512]{1,0:T(8,128)(2,1)} %refs_4_.1, ...), custom_call_target="tpu_custom_call" | custom-call | tf_op jit(solution)/shard_map/pallas_call | solution.py:508
  90.9 1.9 %shard_map.149 = (bf16[128,512]{1,0:T(8,128)(2,1)}, bf16[256,512]{1,0:T(8,128)(2,1)}, bf16[128,512]{1,0:T(8,128)(2,1)}) custom-call(bf16[128,512]{1,0:T(8,128)(2,1)} %get-tuple-element.6.refs_0_, bf16[256,512]{1,0:T(8,128)(2,1)} %get-tuple-element.7.refs_1_, bf16[128,512]{1,0:T(8,128)(2,1)} %get-tuple-element.8.refs_2_), custom_call_target="tpu_custom_call" | custom-call | tf_op jit(solution)/shard_map/pallas_call | solution.py:522
